TPU v7x, 256 devices: a whole 4x4x8 slice. The times are simulated.
256 devices in a mesh: dp: 4 (over x), owner: 64 (over z, y, core).
Axes of the slice: x: 4, y: 4, z: 8, core: 2. Of those that a mesh axis runs over, the one named last changes fastest.
Arguments:
- tokens: bfloat16 [32768, 2048], P(('dp', 'owner')), may hold values from -6 to 6
- grads: bfloat16 [32768, 8, 768], P(('dp', 'owner')), may hold values from -0.19921875 to 0.19921875
- routing: int32 [32768, 8], P(('dp', 'owner')), may hold values from 0 to 127, as said below
- basis_in: bfloat16 [64, 2048, 2048], P('owner'), may hold values from -0.125 to 0.125
- basis_out: bfloat16 [64, 768, 768], P('owner'), may hold values from -0.21875 to 0.21875
Outputs:
- eigenvalues: float32 [2048, 64, 768], P('dp', 'owner')
Inputs may be any that keep to these rules, and one draw needn't show every extreme that they name: `routing`: in each device's block of 128 tokens no expert is chosen by more than 16 tokens, and some expert below 64 is chosen by exactly 16 tokens of every block. The 8 experts of one token differ.
All inputs are finite; a program needn't handle non-finite values.
Results may differ from a plain program's by a relative error of at most 0.00048.
Values may be sent and summed in bfloat16 or wider, within the bound.
No kernel may reach another device: no remote copies, remote signals or barrier semaphores. Data moves between devices by JAX's collectives and lax.ppermute only.
A program may use at most 128 MiB of HBM per device.

v0:
```python
import jax
import jax.numpy as jnp
from jax import lax
from jax.sharding import PartitionSpec as P

CAP = 16


def on_device(tokens, grads, routing, basis_in, basis_out):
    tok_dev, width = tokens.shape
    top = routing.shape[1]
    hidden = grads.shape[2]
    exp_dev = basis_in.shape[0]
    owners = lax.axis_size("owner")
    window = exp_dev * owners
    flat = routing.reshape(-1)
    onehot = (flat[:, None] == jnp.arange(window, dtype=jnp.int32)[None, :]).astype(jnp.int32)
    rank = jnp.sum((jnp.cumsum(onehot, axis=0) - onehot) * onehot, axis=1)
    target = jnp.where(flat < window, flat, window)
    in_rows = jnp.repeat(tokens, top, axis=0)
    out_rows = grads.reshape(tok_dev * top, hidden)
    send_in = (
        jnp.zeros((window, CAP, width), jnp.bfloat16).at[target, rank].set(in_rows, mode="drop")
    )
    send_out = (
        jnp.zeros((window, CAP, hidden), jnp.bfloat16).at[target, rank].set(out_rows, mode="drop")
    )
    recv_in, recv_out = (
        lax.all_to_all(send_in, "owner", split_axis=0, concat_axis=1, tiled=True),
        lax.all_to_all(send_out, "owner", split_axis=0, concat_axis=1, tiled=True),
    )
    rotated_out = jnp.einsum(
        "esf,efk->esk", recv_out, basis_out, preferred_element_type=jnp.float32
    )
    g_sq = (rotated_out * rotated_out).astype(jnp.bfloat16)
    rotated_in = jnp.einsum("esd,edk->esk", recv_in, basis_in, preferred_element_type=jnp.float32)
    a_sq = (rotated_in * rotated_in).astype(jnp.bfloat16)
    quarter = lax.all_to_all(a_sq, "dp", split_axis=2, concat_axis=1, tiled=True)
    all_grads = lax.all_gather(g_sq, "dp", axis=1, tiled=True)
    values = jnp.einsum("esd,esf->def", quarter, all_grads, preferred_element_type=jnp.float32)
    return values


def solution(mesh):
    return jax.shard_map(
        on_device,
        mesh=mesh,
        in_specs=(
            P(("dp", "owner"), None),
            P(("dp", "owner"), None, None),
            P(("dp", "owner"), None),
            P("owner", None, None),
            P("owner", None, None),
        ),
        out_specs=P("dp", "owner", None),
        check_vma=False,
    )
```

profile of v0, /device:TPU:56, one launch (start us, length us, event | category | flops | bytes accessed | tf_op | source)
XLA Modules:
  0.0 346.2 jit_solution(4987443988182270449)
XLA Ops:
  6.5 0.9 copy.21
  7.4 0.1 eq.29
  7.5 0.1 eq.25
  7.6 0.1 reshape.101
  7.8 18.0 %reduce-window.6 = s32[64,8,128]{2,1,0:T(8,128)S(1)} reduce-window(s32[64,8,128]{2,1,0:T(8,128)S(1)} %fusion.18, s32[]{:T(128)} %constant.6.clone.1), window={size=1x1x128 pad=0_0x0_0x127_0}, to_apply=%region_0.0 | reduce-window | flops 8323072 | bytes 524292 | tf_op jit(solution)/shard_map/reduce-window
  25.8 0.1 slice.8
  25.9 0.1 copy.24
  26.1 0.1 copy.25
  26.2 0.1 broadcast_add_fusion
  26.3 0.1 fusion.17
  26.4 0.7 multiply_reduce_fusion
  27.2 0.8 and_reduce_fusion
  27.9 6.4 %scatter_custom_fusion = bf16[1024,768]{1,0:T(8,128)(2,1)} fusion(s32[1024]{0:T(1024)S(1)} %broadcast_select_fusion, bf16[128,8,768]{2,1,0:T(8,128)(2,1)S(1)} %copy-done, bf16[]{:T(256)} %constant.4.clone.1), kind=kCustom, calls=%fused_computation.11 | custom fusion | bytes 3145730
  34.4 11.4 %all-to-all-start = ((bf16[64,16,768]{2,1,0:T(8,128)(2,1)}), bf16[64,16,768]{2,1,0:T(8,128)(2,1)S(1)}, u32[]{:S(2)}, u32[]{:S(2)}) async-start(bf16[64,16,768]{2,1,0:T(8,128)(2,1)} %bitcast.4), calls=%async_computation | async-start | bytes 3145728 | tf_op jit(solution)/shard_map/all_to_all | solution.py:30
  45.8 9.0 %scatter_custom_fusion.1 = bf16[1024,2048]{1,0:T(8,128)(2,1)} fusion(s32[1024]{0:T(1024)S(1)} %broadcast_select_fusion, bf16[]{:T(256)} %constant.4.clone.1, bf16[128,2048]{1,0:T(8,128)(2,1)S(1)} %copy-done.2), kind=kCustom, calls=%fused_computation.5 | custom fusion | bytes 4718594
  54.9 30.2 %all-to-all-done = bf16[64,16,768]{2,1,0:T(8,128)(2,1)S(1)} async-done(((bf16[64,16,768]{2,1,0:T(8,128)(2,1)}), bf16[64,16,768]{2,1,0:T(8,128)(2,1)S(1)}, u32[]{:S(2)}, u32[]{:S(2)}) %all-to-all-start) | async-done | bytes 1572896 | tf_op jit(solution)/shard_map/all_to_all | solution.py:30
  85.0 6.6 %all-to-all-start.1 = ((bf16[64,16,2048]{2,1,0:T(8,128)(2,1)}), bf16[64,16,2048]{2,1,0:T(8,128)(2,1)}, u32[]{:S(2)}, u32[]{:S(2)}) async-start(bf16[64,16,2048]{2,1,0:T(8,128)(2,1)} %bitcast.58), calls=%async_computation.1 | async-start | bytes 8388608 | tf_op jit(solution)/shard_map/all_to_all | solution.py:29
  91.6 0.2 all-gather.3.cloned.1.call-start
  91.9 2.5 multiply_convert_fusion.1
  94.4 0.0 all-gather.3.cloned.1.call-update
  94.4 92.5 %all-to-all-done.1 = bf16[64,16,2048]{2,1,0:T(8,128)(2,1)} async-done(((bf16[64,16,2048]{2,1,0:T(8,128)(2,1)}), bf16[64,16,2048]{2,1,0:T(8,128)(2,1)}, u32[]{:S(2)}, u32[]{:S(2)}) %all-to-all-start.1) | async-done | bytes 4194336 | tf_op jit(solution)/shard_map/all_to_all | solution.py:29
  187.0 13.9 %fusion.6 = bf16[1,1024,2048]{2,1,0:T(8,128)(2,1)} fusion(bf16[1024,2048]{1,0:T(8,128)(2,1)} %bitcast.9, bf16[1,2048,2048]{2,1,0:T(8,128)(2,1)} %param.8), kind=kOutput, calls=%fused_computation.7 | convolution fusion | flops 8594128896 | bytes 16777216 | tf_op jit(solution)/shard_map/esd,edk->esk/dot_general | solution.py:36
  200.8 20.6 %copy.26 = bf16[1,1024,2048]{1,0,2:T(2,128)(2,1)} copy(bf16[1,1024,2048]{2,1,0:T(8,128)(2,1)} %fusion.6) | data formatting | bytes 8388608 | tf_op jit(solution)/shard_map/convert_element_type | solution.py:37
  221.4 0.5 broadcast.100
  221.9 25.9 %reduce.6 = bf16[2048,1024]{1,0:T(8,128)(2,1)} reduce(bf16[2048,1,1024]{2,1,0:T(2,128)(2,1)} %bitcast.55, bf16[]{:T(256)} %broadcast.100), dimensions={1}, to_apply=%bitcast.49.reduce_sub_computation | reduce | bytes 8388610
  247.9 6.2 %reshape.137 = bf16[4,2,262144]{2,1,0:T(2,128)(2,1)} reshape(bf16[2048,1024]{1,0:T(8,128)(2,1)} %reduce.6) | data formatting | bytes 8388608
  254.1 54.9 %all_to_all.33 = bf16[4,2,262144]{2,1,0:T(2,128)(2,1)} all-to-all(bf16[4,2,262144]{2,1,0:T(2,128)(2,1)} %reshape.137), channel_id=1, replica_groups=mesh['dp'=4,'owner'=64] {'dp'}, dimensions={0} | all-to-all | bytes 8388608 | tf_op jit(solution)/shard_map/all_to_all | solution.py:38
  309.0 7.4 %reshape.138 = bf16[2048,1,1024]{2,1,0:T(2,128)(2,1)} reshape(bf16[4,2,262144]{2,1,0:T(2,128)(2,1)} %all_to_all.33) | data formatting | bytes 8388608
  316.4 7.1 %copy.29 = bf16[1,1024,2048]{1,2,0:T(8,128)(2,1)} copy(bf16[1,1024,2048]{1,0,2:T(2,128)(2,1)} %bitcast.56) | data formatting | bytes 8388608
  323.5 6.2 %copy.27 = bf16[1,4,1024,512]{3,2,1,0:T(8,128)(2,1)} copy(bf16[1,4,1024,512]{2,3,1,0:T(8,128)(2,1)} %bitcast.57) | data formatting | bytes 8388608 | tf_op jit(solution)/shard_map/all_to_all | solution.py:38
  329.7 6.9 %convolution_bitcast_fusion = f32[512,1,768]{0,2,1:T(8,128)S(1)} fusion(bf16[4096,768]{1,0:T(8,128)(2,1)} %all-gather.3.cloned.1.call-done, bf16[4096,512]{1,0:T(8,128)(2,1)} %bitcast.59), kind=kOutput, calls=%fused_computation.13 | convolution fusion | flops 3221225472 | bytes 12058624 | tf_op jit(solution)/shard_map/esd,esf->def/dot_general | solution.py:40
  336.6 2.8 copy.28
  (14 shorter events, 0.1 us)
Async XLA Ops:
  6.5 21.4 %copy-start = (bf16[128,8,768]{2,1,0:T(8,128)(2,1)S(1)}, bf16[128,8,768]{2,1,0:T(8,128)(2,1)}, u32[]{:S(2)}) copy-start(bf16[128,8,768]{2,1,0:T(8,128)(2,1)} %param.6) | copy-start | bytes 4718596
  7.8 38.1 %copy-start.2 = (bf16[128,2048]{1,0:T(8,128)(2,1)S(1)}, bf16[128,2048]{1,0:T(8,128)(2,1)}, u32[]{:S(2)}) copy-start(bf16[128,2048]{1,0:T(8,128)(2,1)} %param.5) | copy-start | bytes 1572868
  34.4 50.6 %all-to-all-start = ((bf16[64,16,768]{2,1,0:T(8,128)(2,1)}), bf16[64,16,768]{2,1,0:T(8,128)(2,1)S(1)}, u32[]{:S(2)}, u32[]{:S(2)}) async-start(bf16[64,16,768]{2,1,0:T(8,128)(2,1)} %bitcast.4), calls=%async_computation | async-start | bytes 3145728 | tf_op jit(solution)/shard_map/all_to_all | solution.py:30
  85.0 6.8 %copy-start.3 = (bf16[1,768,768]{2,1,0:T(8,128)(2,1)S(1)}, bf16[1,768,768]{2,1,0:T(8,128)(2,1)}, u32[]{:S(2)}) copy-start(bf16[1,768,768]{2,1,0:T(8,128)(2,1)} %param.9) | copy-start | bytes 3538948
  85.0 101.9 %all-to-all-start.1 = ((bf16[64,16,2048]{2,1,0:T(8,128)(2,1)}), bf16[64,16,2048]{2,1,0:T(8,128)(2,1)}, u32[]{:S(2)}, u32[]{:S(2)}) async-start(bf16[64,16,2048]{2,1,0:T(8,128)(2,1)} %bitcast.58), calls=%async_computation.1 | async-start | bytes 8388608 | tf_op jit(solution)/shard_map/all_to_all | solution.py:29
  91.6 238.1 %all-gather.3.cloned.1.call-start = ((), (), s32[]{:S(2)}) async-start(), calls=%async_computation.3 | async-start | bytes 7864320 | tf_op jit(solution)/shard_map/all_gather | solution.py:39
  329.7 9.7 %copy-start.1 = (bf16[128,8,768]{2,1,0:T(8,128)(2,1)S(1)}, bf16[128,8,768]{2,1,0:T(8,128)(2,1)}, u32[]{:S(2)}) copy-start(bf16[128,8,768]{2,1,0:T(8,128)(2,1)} %param.6) | copy-start | bytes 4718596
Sparse Core Ops, SparseCore 0:
  94.6 69.4 all-gather.2
where the time goes:
time: 347 us; the launch traced here: 346 us
  waiting for transfers between devices  123 us (35%)
  local copies, waits for them, and re-layouts  67.8 us (20%)
  blocking collectives  54.9 us (16%)
  other arithmetic  45.7 us (13%)
  matrix products  23.3 us (7%)
  starting transfers between devices  18.3 us (5%)
  between operations  13.5 us (4%)
    all_to_all x1, waiting for transfers between devices, on_device(): lax.all_to_all(send_in, 'owner', split_axis=0, concat_axis=1, tiled=True)  92.5 us
    all_to_all x1, blocking collectives, on_device(): lax.all_to_all(a_sq, 'dp', split_axis=2, concat_axis=1, tiled=True)  54.9 us
    unnamed x15, local copies, waits for them, and re-layouts  37.7 us
    all_to_all x1, waiting for transfers between devices, on_device(): lax.all_to_all(send_out, 'owner', split_axis=0, concat_axis=1, tiled=True)  30.2 us
    unnamed x4, other arithmetic  27.4 us
    convert_element_type x1, local copies, waits for them, and re-layouts, on_device(): a_sq = (rotated_in * rotated_in).astype(jnp.bfloat16)  20.6 us
    another operation x3, other arithmetic  18.2 us
    dot_general x1, matrix products, on_device(): jnp.einsum('esd,edk->esk', recv_in, basis_in, preferred_element_type=jnp....  13.9 us
  transfers between devices with their start and end apart: 3, of which 2 were waited for; matrix products, arithmetic and copies ran while one was open for 29% of the time, Pallas kernels for 0%

commit v1 on v0

--- a/solution.py
+++ b/solution.py
@@ -35,7 +35,9 @@
     g_sq = (rotated_out * rotated_out).astype(jnp.bfloat16)
     rotated_in = jnp.einsum("esd,edk->esk", recv_in, basis_in, preferred_element_type=jnp.float32)
     a_sq = (rotated_in * rotated_in).astype(jnp.bfloat16)
-    quarter = lax.all_to_all(a_sq, "dp", split_axis=2, concat_axis=1, tiled=True)
+    quarter = jnp.concatenate(
+        lax.all_to_all(jnp.stack(jnp.split(a_sq, lax.axis_size("dp"), axis=2)), "dp", 0, 0), axis=1
+    )
     all_grads = lax.all_gather(g_sq, "dp", axis=1, tiled=True)
     values = jnp.einsum("esd,esf->def", quarter, all_grads, preferred_element_type=jnp.float32)
     return values

time: 347 us -> 270 us (0.78)
  local copies, waits for them, and re-layouts: 67.8 us -> 20.7 us
  other arithmetic: 45.7 us -> 20.3 us
    unnamed x4 -> x3, other arithmetic: 27.4 us -> 1.5 us
    unnamed x15 -> x5, local copies, waits for them, and re-layouts: 37.7 us -> 17 us
    convert_element_type x1 -> x0, local copies, waits for them, and re-layouts: 20.6 us -> none  [on_device(): a_sq = (rotated_in * rotated_in).astype(jnp.bfloat16)]
    all_to_all x1 -> x0, local copies, waits for them, and re-layouts: 6.19 us -> none  [on_device(): lax.all_to_all(a_sq, 'dp', split_axis=2, concat_axis=1, tiled=True)]
    another operation x3 -> x4, other arithmetic: 18.2 us -> 18.8 us
  transfers between devices with their start and end apart: 3 -> 3, of which waited for: 2 -> 2; matrix products, arithmetic and copies ran while one was open for 29% -> 10% of each run, Pallas kernels for 0% -> 0%
where the time goes in v1:
time: 270 us
  waiting for transfers between devices  121 us (45%)
  blocking collectives  53.1 us (20%)
  matrix products  23.1 us (9%)
  local copies, waits for them, and re-layouts  20.7 us (8%)
  other arithmetic  20.3 us (8%)
  starting transfers between devices  18.1 us (7%)
  between operations  13.5 us (5%)
    all_to_all x1, waiting for transfers between devices, on_device(): lax.all_to_all(send_in, 'owner', split_axis=0, concat_axis=1, tiled=True)  91.3 us
    all_to_all x1, blocking collectives, on_device(): lax.all_to_all(jnp.stack(jnp.split(a_sq, lax.axis_size('dp'), axis=2)), '...  53.1 us
    all_to_all x1, waiting for transfers between devices, on_device(): lax.all_to_all(send_out, 'owner', split_axis=0, concat_axis=1, tiled=True)  29.6 us
    another operation x3, other arithmetic  18.2 us
    unnamed x5, local copies, waits for them, and re-layouts  17 us
    dot_general x1, matrix products, on_device(): jnp.einsum('esd,edk->esk', recv_in, basis_in, preferred_element_type=jnp....  12.5 us
    all_to_all x1, starting transfers between devices, on_device(): lax.all_to_all(send_out, 'owner', split_axis=0, concat_axis=1, tiled=True)  11.4 us
    dot_general x1, matrix products, on_device(): jnp.einsum('esd,esf->def', quarter, all_grads, preferred_element_type=jnp...  6.8 us
  transfers between devices with their start and end apart: 3, of which 2 were waited for; matrix products, arithmetic and copies ran while one was open for 10% of the time, Pallas kernels for 0%

profile of v1, /device:TPU:56, one launch (start us, length us, event | category | flops | bytes accessed | tf_op | source)
XLA Modules:
  0.0 269.8 jit_solution(853579221567439363)
XLA Ops:
  6.5 0.0 copy-start
  6.5 0.9 copy.7
  7.4 0.1 eq.29
  7.5 0.1 eq.25
  7.6 0.1 reshape.102
  7.8 18.0 %reduce-window.6 = s32[64,8,128]{2,1,0:T(8,128)S(1)} reduce-window(s32[64,8,128]{2,1,0:T(8,128)S(1)} %fusion.18, s32[]{:T(128)} %constant.6.clone.1), window={size=1x1x128 pad=0_0x0_0x127_0}, to_apply=%region_0.0 | reduce-window | flops 8323072 | bytes 524292 | tf_op jit(solution)/shard_map/reduce-window
  25.8 0.1 slice.8
  25.9 0.1 copy.10
  26.1 0.1 copy.11
  26.2 0.1 broadcast_add_fusion
  26.3 0.1 fusion.17
  26.4 0.7 multiply_reduce_fusion
  27.2 0.8 and_reduce_fusion
  27.9 0.0 copy-done
  27.9 6.4 %scatter_custom_fusion = bf16[1024,768]{1,0:T(8,128)(2,1)} fusion(s32[1024]{0:T(1024)S(1)} %broadcast_select_fusion, bf16[128,8,768]{2,1,0:T(8,128)(2,1)S(1)} %copy-done, bf16[]{:T(256)} %constant.4.clone.1), kind=kCustom, calls=%fused_computation.12 | custom fusion | bytes 3145730
  34.4 11.4 %all-to-all-start = ((bf16[64,16,768]{2,1,0:T(8,128)(2,1)}), bf16[64,16,768]{2,1,0:T(8,128)(2,1)S(1)}, u32[]{:S(2)}, u32[]{:S(2)}) async-start(bf16[64,16,768]{2,1,0:T(8,128)(2,1)} %bitcast.4), calls=%async_computation | async-start | bytes 3145728 | tf_op jit(solution)/shard_map/all_to_all | solution.py:30
  45.8 9.6 %scatter_custom_fusion.1 = bf16[1024,2048]{1,0:T(8,128)(2,1)} fusion(s32[1024]{0:T(1024)S(1)} %broadcast_select_fusion, bf16[]{:T(256)} %constant.4.clone.1, bf16[128,2048]{1,0:T(8,128)(2,1)} %param.5), kind=kCustom, calls=%fused_computation.6 | custom fusion | bytes 4718594
  55.4 29.6 %all-to-all-done = bf16[64,16,768]{2,1,0:T(8,128)(2,1)S(1)} async-done(((bf16[64,16,768]{2,1,0:T(8,128)(2,1)}), bf16[64,16,768]{2,1,0:T(8,128)(2,1)S(1)}, u32[]{:S(2)}, u32[]{:S(2)}) %all-to-all-start) | async-done | bytes 1572896 | tf_op jit(solution)/shard_map/all_to_all | solution.py:30
  85.0 6.5 %all-to-all-start.1 = ((bf16[64,16,2048]{2,1,0:T(8,128)(2,1)}), bf16[64,16,2048]{2,1,0:T(8,128)(2,1)}, u32[]{:S(2)}, u32[]{:S(2)}) async-start(bf16[64,16,2048]{2,1,0:T(8,128)(2,1)} %bitcast.58), calls=%async_computation.1 | async-start | bytes 8388608 | tf_op jit(solution)/shard_map/all_to_all | solution.py:29
  91.5 0.2 all-gather.3.cloned.1.call-start
  91.7 3.8 %multiply_convert_fusion.1 = bf16[1024,768]{1,0:T(8,128)(2,1)} fusion(bf16[1024,768]{1,0:T(8,128)(2,1)S(1)} %bitcast.60, bf16[1,768,768]{2,1,0:T(8,128)(2,1)} %param.9), kind=kOutput, calls=%fused_computation.9 | convolution fusion | flops 1209532416 | bytes 4325376 | tf_op jit(solution)/shard_map/esf,efk->esk/dot_general | solution.py:32
  95.5 0.0 all-gather.3.cloned.1.call-update
  95.6 91.3 %all-to-all-done.1 = bf16[64,16,2048]{2,1,0:T(8,128)(2,1)} async-done(((bf16[64,16,2048]{2,1,0:T(8,128)(2,1)}), bf16[64,16,2048]{2,1,0:T(8,128)(2,1)}, u32[]{:S(2)}, u32[]{:S(2)}) %all-to-all-start.1) | async-done | bytes 4194336 | tf_op jit(solution)/shard_map/all_to_all | solution.py:29
  186.8 12.5 %fusion.6 = bf16[1,1024,2048]{2,1,0:T(8,128)(2,1)S(1)} fusion(bf16[1024,2048]{1,0:T(8,128)(2,1)} %bitcast.9, bf16[1,2048,2048]{2,1,0:T(8,128)(2,1)} %param.8), kind=kOutput, calls=%fused_computation.8 | convolution fusion | flops 8594128896 | bytes 16777216 | tf_op jit(solution)/shard_map/esd,edk->esk/dot_general | solution.py:36
  199.3 0.4 slice_bitcast_fusion.3
  199.7 0.6 pad_maximum_fusion
  200.3 53.1 %all_to_all.23 = bf16[4,1,1024,512]{3,2,1,0:T(8,128)(2,1)} all-to-all(bf16[4,1,1024,512]{3,2,1,0:T(8,128)(2,1)S(1)} %pad_maximum_fusion), channel_id=1, replica_groups=mesh['dp'=4,'owner'=64] {'dp'}, dimensions={0} | all-to-all | bytes 8388608 | tf_op jit(solution)/shard_map/all_to_all | solution.py:39
  253.4 0.0 all-gather.3.cloned.1.call-done
  253.4 6.8 %convolution_bitcast_fusion = f32[512,1,768]{0,2,1:T(8,128)S(1)} fusion(bf16[4096,768]{1,0:T(8,128)(2,1)} %all-gather.3.cloned.1.call-done, bf16[4096,512]{1,0:T(8,128)(2,1)} %bitcast.59), kind=kOutput, calls=%fused_computation.14 | convolution fusion | flops 3221225472 | bytes 12058624 | tf_op jit(solution)/shard_map/esd,esf->def/dot_general | solution.py:42
  260.2 2.8 %copy.12 = f32[512,1,768]{2,1,0:T(1,128)} copy(f32[512,1,768]{0,2,1:T(8,128)S(1)} %convolution_bitcast_fusion) | data formatting | bytes 3145728 | tf_op jit(solution)/shard_map/esd,esf->def/transpose | solution.py:42
  (5 shorter events, 0.1 us)
Async XLA Ops:
  6.5 21.4 %copy-start = (bf16[128,8,768]{2,1,0:T(8,128)(2,1)S(1)}, bf16[128,8,768]{2,1,0:T(8,128)(2,1)}, u32[]{:S(2)}) copy-start(bf16[128,8,768]{2,1,0:T(8,128)(2,1)} %param.6) | copy-start | bytes 4718596
  34.4 50.6 %all-to-all-start = ((bf16[64,16,768]{2,1,0:T(8,128)(2,1)}), bf16[64,16,768]{2,1,0:T(8,128)(2,1)S(1)}, u32[]{:S(2)}, u32[]{:S(2)}) async-start(bf16[64,16,768]{2,1,0:T(8,128)(2,1)} %bitcast.4), calls=%async_computation | async-start | bytes 3145728 | tf_op jit(solution)/shard_map/all_to_all | solution.py:30
  85.0 101.8 %all-to-all-start.1 = ((bf16[64,16,2048]{2,1,0:T(8,128)(2,1)}), bf16[64,16,2048]{2,1,0:T(8,128)(2,1)}, u32[]{:S(2)}, u32[]{:S(2)}) async-start(bf16[64,16,2048]{2,1,0:T(8,128)(2,1)} %bitcast.58), calls=%async_computation.1 | async-start | bytes 8388608 | tf_op jit(solution)/shard_map/all_to_all | solution.py:29
  91.5 161.9 %all-gather.3.cloned.1.call-start = ((), (), s32[]{:S(2)}) async-start(), calls=%async_computation.3 | async-start | bytes 7864320 | tf_op jit(solution)/shard_map/all_gather | solution.py:41
Sparse Core Ops, SparseCore 0:
  95.7 69.4 all-gather.2
